TPU v7x, 32 devices: a whole 2x2x4 slice. The times are simulated.
32 devices in a mesh: groups: 2 (over x), lat: 16 (over z, y, core).
Axes of the slice: x: 2, y: 2, z: 4, core: 2. Of those that a mesh axis runs over, the one named last changes fastest.
Arguments:
- field: bfloat16 [64, 128, 2688], P(('groups', 'lat')), parts along dimension 0, may hold values from -6 to 6
- target: bfloat16 [64, 128, 2688], P(('groups', 'lat')), parts along dimension 0, may hold values from -6 to 6
- cycle_len: int32 [32], replicated, may hold values from 20 to 2568, as said below
- legendre: bfloat16 [640, 32, 640], P('lat'), may hold values from -1 to 1
- spectral_filter: float32 [640, 128], replicated, may hold values from -4 to 4
Outputs:
- errors: bfloat16 [64, 128, 2688], P(('groups', 'lat')), parts along dimension 0
- grad_filter: float32 [1280, 128], P('groups'), parts along dimension 0
There are 2 independent parts, one for each index of `groups`. A program takes and returns all parts, laid end to end along the dimension named above; an argument that names none is the same for every part. Nothing has to cross between parts.
Inputs may be any that keep to these rules, and one draw needn't show every extreme that they name: `cycle_len`: the cycles nearest the equator have exactly 2568 points and the polar cycles 20; every length is 20 plus a multiple of 4, and lengths fall from the equator toward both poles but for small steps.
All inputs are finite; a program needn't handle non-finite values.
Results may differ from a plain program's by a relative error of at most 0.0079.
Values may be sent and summed in bfloat16 or wider, within the bound.
A program may use at most 256 MiB of HBM per device.

v0:
```python
import math

import jax
import jax.numpy as jnp
from jax import lax
from jax.sharding import PartitionSpec as P

MM = 640
LL = 640
LPAD = 2688
HALF = 1288


def fold_table(length, amount, upper_col):
    columns = jnp.arange(amount, dtype=jnp.int32)
    wavenum = jnp.arange(MM, dtype=jnp.int32)
    half_len = length // 2
    phases = wavenum[:, None] * columns[None, :] % length
    angles = 2.0 * math.pi * phases.astype(jnp.float32) / length.astype(jnp.float32)
    inside = (
        (columns[None, :] < upper_col)
        & (columns[None, :] <= half_len)
        & (wavenum[:, None] < half_len)
    )
    cosine = jnp.where(inside, jnp.cos(angles), 0.0).astype(jnp.bfloat16)
    sine_part = jnp.where(inside, jnp.sin(angles), 0.0).astype(jnp.bfloat16)
    return jnp.stack([cosine, sine_part])


def mirror_cols(values, length, width_out):
    blank = jnp.zeros((values.shape[0], width_out), values.dtype)
    extended = jnp.concatenate([blank, values[:, ::-1], blank], axis=1)
    start_col = width_out + values.shape[1] - 1 - length
    return lax.dynamic_slice_in_dim(extended, start_col, width_out, 1)


def fold_cycle(values, length):
    half_len = length // 2
    direct = values[:, :HALF].astype(jnp.float32)
    mirrored = mirror_cols(values, length, HALF).astype(jnp.float32)
    col_index = jnp.arange(HALF, dtype=jnp.int32)[None, :]
    middle = (col_index >= 1) & (col_index < half_len)
    rim_cols = (col_index == 0) | (col_index == half_len)
    even_part = jnp.where(middle, direct + mirrored, jnp.where(rim_cols, direct, 0.0)).astype(
        jnp.bfloat16
    )
    odd_part = jnp.where(middle, direct - mirrored, 0.0).astype(jnp.bfloat16)
    return (even_part, odd_part)


def unfold_cycle(cos_part, sin_part, length):
    half_len = length // 2
    front_part = jnp.concatenate(
        [cos_part - sin_part, jnp.zeros((cos_part.shape[0], LPAD - HALF), cos_part.dtype)], axis=1
    )
    mirrored = mirror_cols(cos_part + sin_part, length, LPAD)
    columns = jnp.arange(LPAD, dtype=jnp.int32)[None, :]
    return jnp.where(columns <= half_len, front_part, jnp.where(columns < length, mirrored, 0.0))


def local(field, target, cycle_len, legendre, spectral_filter):
    cycle_count, chan_count, col_count = field.shape
    position = lax.axis_index("lat")
    mode_local = legendre.shape[0]
    sign_pair = jnp.array([1.0, -1.0], dtype=jnp.float32)[:, None, None]
    wavenum = jnp.arange(MM, dtype=jnp.int32)
    doubled = jnp.where(wavenum == 0, 1.0, 2.0).astype(jnp.float32)[None, :, None]
    columns = jnp.arange(col_count, dtype=jnp.int32)
    own_len = lax.dynamic_slice_in_dim(cycle_len, position * cycle_count, cycle_count)
    tables = [fold_table(own_len[member], HALF, HALF) for member in range(cycle_count)]

    def analyse_cycles(even_all, odd_all):
        return jnp.stack(
            [
                jnp.stack(
                    [
                        jnp.einsum(
                            "mk,ck->mc",
                            tables[member][0],
                            even_all[member],
                            preferred_element_type=jnp.float32,
                        ),
                        jnp.einsum(
                            "mk,ck->mc",
                            tables[member][1],
                            odd_all[member],
                            preferred_element_type=jnp.float32,
                        ),
                    ]
                )
                for member in range(cycle_count)
            ]
        )

    def synth_cycles(weighted):
        return jnp.stack(
            [
                jnp.stack(
                    [
                        jnp.einsum(
                            "mc,mk->ck",
                            weighted[member][0],
                            tables[member][0],
                            preferred_element_type=jnp.float32,
                        ),
                        jnp.einsum(
                            "mc,mk->ck",
                            weighted[member][1],
                            tables[member][1],
                            preferred_element_type=jnp.float32,
                        ),
                    ]
                )
                for member in range(cycle_count)
            ]
        )

    folded = [fold_cycle(field[member], own_len[member]) for member in range(cycle_count)]
    totals = analyse_cycles(
        jnp.stack([pair[0] for pair in folded]), jnp.stack([pair[1] for pair in folded])
    )
    coeffs = (totals * sign_pair[None] / own_len.astype(jnp.float32)[:, None, None, None]).astype(
        jnp.bfloat16
    )
    gathered = lax.all_to_all(coeffs, "lat", split_axis=2, concat_axis=0, tiled=True)
    mode_ids = position * mode_local + jnp.arange(mode_local, dtype=jnp.int32)
    degrees = jnp.arange(LL, dtype=jnp.int32)
    keeper = (degrees[None, :] >= mode_ids[:, None]).astype(jnp.float32)[:, :, None, None]
    gain_table = keeper * spectral_filter[None, :, None, :]
    amplitude = jnp.einsum("mrl,rpmc->mlpc", legendre, gathered, preferred_element_type=jnp.float32)
    filtered = (amplitude * gain_table).astype(jnp.bfloat16)
    synth_modes = jnp.einsum(
        "mrl,mlpc->rpmc", legendre, filtered, preferred_element_type=jnp.float32
    ).astype(jnp.bfloat16)
    synth_back = lax.all_to_all(synth_modes, "lat", split_axis=0, concat_axis=2, tiled=True)
    weighted = (synth_back.astype(jnp.float32) * doubled[None]).astype(jnp.bfloat16)
    parts_all = synth_cycles(weighted)
    error_list = []
    for member in range(cycle_count):
        output = unfold_cycle(parts_all[member, 0], parts_all[member, 1], own_len[member])
        error_list.append(
            jnp.where(
                columns[None, :] < own_len[member], output - target[member].astype(jnp.float32), 0.0
            ).astype(jnp.bfloat16)
        )
    errors = jnp.stack(error_list)
    err_folded = [fold_cycle(errors[member], own_len[member]) for member in range(cycle_count)]
    grad_totals = analyse_cycles(
        jnp.stack([pair[0] for pair in err_folded]), jnp.stack([pair[1] for pair in err_folded])
    )
    grad_coeffs = (grad_totals * sign_pair[None] * doubled[None]).astype(jnp.bfloat16)
    grad_gathered = lax.all_to_all(grad_coeffs, "lat", split_axis=2, concat_axis=0, tiled=True)
    grad_amp = jnp.einsum(
        "mrl,rpmc->mlpc", legendre, grad_gathered, preferred_element_type=jnp.float32
    )
    filter_term = jnp.sum(amplitude * grad_amp * keeper, axis=(0, 2))
    grad_filter = lax.psum(filter_term, "lat")
    return (errors, grad_filter)


def solution(mesh):
    return jax.shard_map(
        local,
        mesh=mesh,
        in_specs=(
            P(("groups", "lat"), None, None),
            P(("groups", "lat"), None, None),
            P(),
            P("lat", None, None),
            P(),
        ),
        out_specs=(P(("groups", "lat"), None, None), P("groups", None)),
        check_vma=False,
    )
```

profile of v0, /device:TPU:0, one launch (start us, length us, event | category | flops | bytes accessed | tf_op | source)
XLA Modules:
  0.0 877.1 jit_solution(10932679594027949728)
XLA Ops:
  7.2 0.9 fusion.239
  18.6 2.3 fusion.241
  20.9 1.4 copy.34
  22.3 6.9 rev.18
  29.3 51.2 %fusion.109 = f32[1,640,128]{2,1,0:T(8,128)} fusion(f32[]{:T(128)S(6)} %convert_element_type.130, pred[]{:T(512)S(6)} %lt.118, s32[]{:T(128)S(6)} %select_n.128, pred[1288]{0:T(1024)(128)(4,1)S(1)} %fusion.193, pred[640]{0:T(1024)(128)(4,1)S(1)} %iota_compare_fusion.16, pred[1288]{0:T(1024)(128)(4,1)S(1)} %get-tuple-element.21, ...), kind=kOutput, calls=%fused_computation.118 | convolution fusion | flops 224215040 | bytes 1680397 | tf_op jit(solution)/shard_map/mk,ck->mc/dot_general | solution.py:83
  80.5 52.1 %fusion.103 = f32[1,640,128]{2,1,0:T(8,128)} fusion(f32[]{:T(128)S(6)} %convert_element_type.130, pred[]{:T(512)S(6)} %lt.118, s32[]{:T(128)S(6)} %select_n.128, pred[1288]{0:T(1024)(128)(4,1)S(1)} %fusion.193, pred[640]{0:T(1024)(128)(4,1)S(1)} %iota_compare_fusion.16, pred[1288]{0:T(1024)(128)(4,1)S(1)} %get-tuple-element.20, ...), kind=kOutput, calls=%fused_computation.116 | convolution fusion | flops 224379904 | bytes 1682445 | tf_op jit(solution)/shard_map/mk,ck->mc/dot_general | solution.py:77
  133.5 0.7 rev.19
  134.2 49.9 %fusion.121 = f32[1,640,128]{2,1,0:T(8,128)S(1)} fusion(f32[]{:T(128)S(6)} %convert_element_type.138, pred[]{:T(512)S(6)} %lt.124, s32[]{:T(128)S(6)} %select_n.137, pred[1288]{0:T(1024)(128)(4,1)S(1)} %fusion.192, pred[640]{0:T(1024)(128)(4,1)S(1)} %iota_compare_fusion.15, pred[1288]{0:T(1024)(128)(4,1)S(1)} %get-tuple-element.23, ...), kind=kOutput, calls=%fused_computation.122 | convolution fusion | flops 224215040 | bytes 1680397 | tf_op jit(solution)/shard_map/mk,ck->mc/dot_general | solution.py:83
  184.2 50.3 %fusion.115 = f32[1,640,128]{2,1,0:T(8,128)S(1)} fusion(f32[]{:T(128)S(6)} %convert_element_type.138, pred[]{:T(512)S(6)} %lt.124, s32[]{:T(128)S(6)} %select_n.137, pred[1288]{0:T(1024)(128)(4,1)S(1)} %fusion.192, pred[640]{0:T(1024)(128)(4,1)S(1)} %iota_compare_fusion.15, pred[1288]{0:T(1024)(128)(4,1)S(1)} %get-tuple-element.22, ...), kind=kOutput, calls=%fused_computation.120 | convolution fusion | flops 224379904 | bytes 1682445 | tf_op jit(solution)/shard_map/mk,ck->mc/dot_general | solution.py:77
  234.9 1.5 copy.20
  236.4 7.6 all-to-all-start
  244.2 6.2 broadcast_multiply_fusion
  250.5 10.1 %all-to-all-done = bf16[2,2,640,128]{3,1,0,2:T(2,128)(2,1)S(1)} async-done(((bf16[2,2,640,128]{3,1,0,2:T(2,128)(2,1)}), bf16[2,2,640,128]{3,1,0,2:T(2,128)(2,1)S(1)}, u32[]{:S(2)}, u32[]{:S(2)}) %all-to-all-start) | async-done | bytes 655392 | tf_op jit(solution)/shard_map/all_to_all | solution.py:125
  260.6 0.6 copy.21
  261.2 10.6 %fusion.72 = f32[40,2,128,640]{3,2,1,0:T(8,128)} fusion(bf16[32,2,40,128]{3,0,1,2:T(8,128)(2,1)S(1)} %bitcast.119, bf16[40,32,640]{2,1,0:T(8,128)(2,1)S(1)} %copy-done), kind=kOutput, calls=%fused_computation.83 | convolution fusion | flops 419430400 | bytes 28508160 | tf_op jit(solution)/shard_map/mrl,rpmc->mlpc/dot_general | solution.py:130
  271.8 14.3 %fusion.98 = bf16[32,2,40,128]{3,0,1,2:T(8,128)(2,1)S(1)} fusion(bf16[40,32,640]{2,1,0:T(8,128)(2,1)S(1)} %copy-done, f32[40,2,128,640]{3,2,1,0:T(8,128)} %fusion.72, f32[40,640,128]{1,2,0:T(8,128)} %broadcast_multiply_fusion), kind=kOutput, calls=%fused_computation.115 | convolution fusion | flops 432865280 | bytes 41615360 | tf_op jit(solution)/shard_map/mrl,mlpc->rpmc/dot_general | solution.py:132
  286.1 1.3 copy.24
  287.5 4.8 all-to-all-start.1
  293.9 1.4 fusion.240
  295.3 1.1 copy.36
  296.5 1.1 copy.37
  297.6 0.6 iota_compare_fusion.1
  298.8 10.2 %all-to-all-done.1 = bf16[32,2,40,128]{3,1,2,0:T(2,128)(2,1)} async-done(((bf16[32,2,40,128]{3,1,2,0:T(2,128)(2,1)}), bf16[32,2,40,128]{3,1,2,0:T(2,128)(2,1)}, u32[]{:S(2)}, u32[]{:S(2)}) %all-to-all-start.1) | async-done | bytes 655392 | tf_op jit(solution)/shard_map/all_to_all | solution.py:135
  309.0 1.2 copy.25
  310.3 48.7 %convolution_bitcast_fusion = f32[1,128,1288]{1,2,0:T(8,128)S(1)} fusion(f32[]{:T(128)S(6)} %convert_element_type.138, pred[]{:T(512)S(6)} %lt.124, s32[]{:T(128)S(6)} %select_n.137, pred[1288]{0:T(1024)(128)(4,1)S(1)} %fusion.192, pred[640]{0:T(1024)(128)(4,1)S(1)} %iota_compare_fusion.15, bf16[2,2,640,128]{3,2,1,0:T(8,128)(2,1)S(1)} %fusion.97), kind=kOutput, calls=%fused_computation.41 | convolution fusion | flops 222566400 | bytes 826377 | tf_op jit(solution)/shard_map/mc,mk->ck/dot_general | solution.py:106
  359.1 48.7 %convolution_bitcast_fusion.1 = f32[1,128,1288]{1,2,0:T(8,128)S(1)} fusion(f32[]{:T(128)S(6)} %convert_element_type.138, pred[]{:T(512)S(6)} %lt.124, s32[]{:T(128)S(6)} %select_n.137, pred[1288]{0:T(1024)(128)(4,1)S(1)} %fusion.192, pred[640]{0:T(1024)(128)(4,1)S(1)} %iota_compare_fusion.15, bf16[2,2,640,128]{3,2,1,0:T(8,128)(2,1)S(1)} %fusion.97), kind=kOutput, calls=%fused_computation.42 | convolution fusion | flops 222566400 | bytes 826377 | tf_op jit(solution)/shard_map/mc,mk->ck/dot_general | solution.py:100
  407.7 48.9 %convolution_bitcast_fusion.3 = f32[1,128,1288]{1,2,0:T(8,128)S(1)} fusion(f32[]{:T(128)S(6)} %convert_element_type.130, pred[]{:T(512)S(6)} %lt.118, s32[]{:T(128)S(6)} %select_n.128, pred[1288]{0:T(1024)(128)(4,1)S(1)} %fusion.193, pred[640]{0:T(1024)(128)(4,1)S(1)} %iota_compare_fusion.16, bf16[2,2,640,128]{3,2,1,0:T(8,128)(2,1)S(1)} %fusion.97), kind=kOutput, calls=%fused_computation.44 | convolution fusion | flops 222566400 | bytes 826377 | tf_op jit(solution)/shard_map/mc,mk->ck/dot_general | solution.py:100
  456.6 49.6 %convolution_bitcast_fusion.2 = f32[1,128,1288]{1,2,0:T(8,128)} fusion(f32[]{:T(128)S(6)} %convert_element_type.130, pred[]{:T(512)S(6)} %lt.118, s32[]{:T(128)S(6)} %select_n.128, pred[1288]{0:T(1024)(128)(4,1)S(1)} %fusion.193, pred[640]{0:T(1024)(128)(4,1)S(1)} %iota_compare_fusion.16, bf16[2,2,640,128]{3,2,1,0:T(8,128)(2,1)S(1)} %fusion.97), kind=kOutput, calls=%fused_computation.43 | convolution fusion | flops 222566400 | bytes 826377 | tf_op jit(solution)/shard_map/mc,mk->ck/dot_general | solution.py:106
  506.3 1.0 subtract_bitcast_fusion
  507.3 3.7 rev.21
  511.0 1.2 maximum_bitcast_fusion
  512.2 0.9 subtract_bitcast_fusion.1
  513.1 3.8 rev.20
  517.0 7.7 fusion.87
  524.6 7.1 rev.22
  531.8 51.6 %fusion.106 = f32[1,640,128]{2,1,0:T(8,128)} fusion(f32[]{:T(128)S(6)} %convert_element_type.130, pred[]{:T(512)S(6)} %lt.118, s32[]{:T(128)S(6)} %select_n.128, pred[1288]{0:T(1024)(128)(4,1)S(1)} %fusion.193, pred[640]{0:T(1024)(128)(4,1)S(1)} %iota_compare_fusion.16, pred[1288]{0:T(1024)(128)(4,1)S(1)} %get-tuple-element.20, ...), kind=kOutput, calls=%fused_computation.117 | convolution fusion | flops 224379904 | bytes 1682445 | tf_op jit(solution)/shard_map/mk,ck->mc/dot_general | solution.py:77
  583.4 51.2 %fusion.112 = f32[1,640,128]{2,1,0:T(8,128)} fusion(f32[]{:T(128)S(6)} %convert_element_type.130, pred[]{:T(512)S(6)} %lt.118, s32[]{:T(128)S(6)} %select_n.128, pred[1288]{0:T(1024)(128)(4,1)S(1)} %fusion.193, pred[640]{0:T(1024)(128)(4,1)S(1)} %iota_compare_fusion.16, pred[1288]{0:T(1024)(128)(4,1)S(1)} %get-tuple-element.21, ...), kind=kOutput, calls=%fused_computation.119 | convolution fusion | flops 224215040 | bytes 1680397 | tf_op jit(solution)/shard_map/mk,ck->mc/dot_general | solution.py:83
  634.6 6.9 rev.23
  641.5 50.9 %fusion.118 = f32[1,640,128]{2,1,0:T(8,128)S(1)} fusion(f32[]{:T(128)S(6)} %convert_element_type.138, pred[]{:T(512)S(6)} %lt.124, s32[]{:T(128)S(6)} %select_n.137, pred[1288]{0:T(1024)(128)(4,1)S(1)} %fusion.192, pred[640]{0:T(1024)(128)(4,1)S(1)} %iota_compare_fusion.15, pred[1288]{0:T(1024)(128)(4,1)S(1)} %get-tuple-element.22, ...), kind=kOutput, calls=%fused_computation.121 | convolution fusion | flops 224379904 | bytes 1682445 | tf_op jit(solution)/shard_map/mk,ck->mc/dot_general | solution.py:77
  692.5 49.7 %fusion.124 = f32[1,640,128]{2,1,0:T(8,128)S(1)} fusion(f32[]{:T(128)S(6)} %convert_element_type.138, pred[]{:T(512)S(6)} %lt.124, s32[]{:T(128)S(6)} %select_n.137, pred[1288]{0:T(1024)(128)(4,1)S(1)} %fusion.192, pred[640]{0:T(1024)(128)(4,1)S(1)} %iota_compare_fusion.15, pred[1288]{0:T(1024)(128)(4,1)S(1)} %get-tuple-element.23, ...), kind=kOutput, calls=%fused_computation.123 | convolution fusion | flops 224215040 | bytes 1680397 | tf_op jit(solution)/shard_map/mk,ck->mc/dot_general | solution.py:83
  742.6 0.7 copy.28
  743.3 23.2 %all_to_all.45 = bf16[2,2,640,128]{3,1,0,2:T(2,128)(2,1)S(1)} all-to-all(bf16[2,2,640,128]{3,1,0,2:T(2,128)(2,1)S(1)} %copy.28), channel_id=1, replica_groups=mesh['groups'=2,'lat'=16] {'lat'}, dimensions={2} | all-to-all | bytes 1310720 | tf_op jit(solution)/shard_map/all_to_all | solution.py:152
  766.5 1.5 copy.29
  767.9 13.0 %fusion.1 = f32[640,128]{0,1:T(8,128)} fusion(f32[40,2,128,640]{3,2,1,0:T(8,128)} %fusion.72, f32[40,640]{1,0:T(8,128)S(1)} %fusion.187, bf16[32,2,40,128]{3,0,1,2:T(8,128)(2,1)} %bitcast.128, bf16[40,32,640]{2,1,0:T(8,128)(2,1)S(1)} %copy-done), kind=kOutput, calls=%fused_computation.2 | convolution fusion | flops 439009280 | bytes 28938240 | tf_op jit(solution)/shard_map/mrl,rpmc->mlpc/dot_general | solution.py:153
  781.0 1.2 pad_maximum_fusion
  782.2 2.5 copy.30
  784.7 83.5 %all-reduce.4.cloned.1.call-done = f32[640,128]{0,1:T(8,128)} async-done(((f32[640,128]{0,1:T(8,128)}), f32[640,128]{0,1:T(8,128)}) %all-reduce.4.cloned.1.call-update) | async-done | bytes 327696 | tf_op jit(solution)/shard_map/psum | solution.py:157
  868.3 1.9 copy.31
  (45 shorter events, 3.3 us)
Async XLA Ops:
  7.2 254.0 %copy-start = (bf16[40,32,640]{2,1,0:T(8,128)(2,1)S(1)}, bf16[40,32,640]{2,1,0:T(8,128)(2,1)}, u32[]{:S(2)}) copy-start(bf16[40,32,640]{2,1,0:T(8,128)(2,1)} %param.9) | copy-start | bytes 4915204
  29.3 51.2 %copy-start.3 = (bf16[128,2688]{0,1:T(8,128)(2,1)S(1)}, bf16[128,2688]{0,1:T(8,128)(2,1)}, u32[]{:S(2)}) copy-start(bf16[128,2688]{0,1:T(8,128)(2,1)} %rev.18) | copy-start | bytes 2064388
  184.2 50.3 %copy-start.6 = (f32[1,640,128]{2,1,0:T(8,128)S(1)}, f32[1,640,128]{2,1,0:T(8,128)}, u32[]{:S(2)}) copy-start(f32[1,640,128]{2,1,0:T(8,128)} %fusion.109) | copy-start | bytes 983044
  184.2 50.3 %copy-start.7 = (f32[1,640,128]{2,1,0:T(8,128)S(1)}, f32[1,640,128]{2,1,0:T(8,128)}, u32[]{:S(2)}) copy-start(f32[1,640,128]{2,1,0:T(8,128)} %fusion.103) | copy-start | bytes 983044
  184.2 50.4 %copy-start.9 = (f32[2]{0:T(128)S(1)}, f32[2]{0:T(128)}, u32[]{:S(2)}) copy-start(f32[2]{0:T(128)} %constant.81.clone) | copy-start | bytes 28
  234.5 9.5 %copy-start.8 = (f32[640,128]{1,0:T(8,128)S(1)}, f32[640,128]{1,0:T(8,128)}, u32[]{:S(2)}) copy-start(f32[640,128]{1,0:T(8,128)} %param.10) | copy-start | bytes 983044
  236.4 24.2 %all-to-all-start = ((bf16[2,2,640,128]{3,1,0,2:T(2,128)(2,1)}), bf16[2,2,640,128]{3,1,0,2:T(2,128)(2,1)S(1)}, u32[]{:S(2)}, u32[]{:S(2)}) async-start(bf16[2,2,640,128]{3,1,0,2:T(2,128)(2,1)} %copy.20), calls=%async_computation | async-start | bytes 1310720 | tf_op jit(solution)/shard_map/all_to_all | solution.py:125
  287.5 21.5 %all-to-all-start.1 = ((bf16[32,2,40,128]{3,1,2,0:T(2,128)(2,1)}), bf16[32,2,40,128]{3,1,2,0:T(2,128)(2,1)}, u32[]{:S(2)}, u32[]{:S(2)}) async-start(bf16[32,2,40,128]{3,1,2,0:T(2,128)(2,1)} %copy.24), calls=%async_computation.1 | async-start | bytes 1310720 | tf_op jit(solution)/shard_map/all_to_all | solution.py:135
  292.3 576.0 %all-reduce.4.cloned.1.call-start = ((), (), s32[]{:S(2)}) async-start(), calls=%async_computation.3 | async-start | bytes 655360 | tf_op jit(solution)/shard_map/psum | solution.py:157
  531.8 51.6 %copy-start.2 = (bf16[128,2688]{0,1:T(8,128)(2,1)S(1)}, bf16[128,2688]{0,1:T(8,128)(2,1)}, u32[]{:S(2)}) copy-start(bf16[128,2688]{0,1:T(8,128)(2,1)} %rev.22) | copy-start | bytes 2064388
  641.5 50.9 %copy-start.1 = (bf16[128,2688]{0,1:T(8,128)(2,1)S(1)}, bf16[128,2688]{0,1:T(8,128)(2,1)}, u32[]{:S(2)}) copy-start(bf16[128,2688]{0,1:T(8,128)(2,1)} %rev.23) | copy-start | bytes 2064388
  692.5 49.7 %copy-start.4 = (f32[1,640,128]{2,1,0:T(8,128)S(1)}, f32[1,640,128]{2,1,0:T(8,128)}, u32[]{:S(2)}) copy-start(f32[1,640,128]{2,1,0:T(8,128)} %fusion.106) | copy-start | bytes 983044
  692.5 49.7 %copy-start.5 = (f32[1,640,128]{2,1,0:T(8,128)S(1)}, f32[1,640,128]{2,1,0:T(8,128)}, u32[]{:S(2)}) copy-start(f32[1,640,128]{2,1,0:T(8,128)} %fusion.112) | copy-start | bytes 983044
Sparse Core Ops, SparseCore 0:
  781.1 87.0 all-reduce.3
where the time goes:
time: 888 us; the launch traced here: 877 us
  matrix products  641 us (72%)
  waiting for transfers between devices  104 us (12%)
  local copies, waits for them, and re-layouts  49 us (6%)
  between operations  26.3 us (3%)
  blocking collectives  23.2 us (3%)
  other arithmetic  21.2 us (2%)
  starting transfers between devices  12.9 us (1%)
    dot_general x4, matrix products, analyse_cycles(): jnp.einsum('mk,ck->mc', tables[member][0], even_all[member], preferred_el...  205 us
    dot_general x4, matrix products, analyse_cycles(): jnp.einsum('mk,ck->mc', tables[member][1], odd_all[member], preferred_ele...  202 us
    dot_general x2, matrix products, synth_cycles(): jnp.einsum('mc,mk->ck', weighted[member][1], tables[member][1], preferred...  98.3 us
    dot_general x2, matrix products, synth_cycles(): jnp.einsum('mc,mk->ck', weighted[member][0], tables[member][0], preferred...  97.6 us
    psum x1, waiting for transfers between devices, local(): grad_filter = lax.psum(filter_term, 'lat')  83.5 us
    rev x6, local copies, waits for them, and re-layouts, mirror_cols(): extended = jnp.concatenate([blank, values[:, ::-1], blank], axis=1)  29.2 us
    all_to_all x1, blocking collectives, local(): lax.all_to_all(grad_coeffs, 'lat', split_axis=2, concat_axis=0, tiled=True)  23.2 us
  transfers between devices with their start and end apart: 3, of which 3 were waited for; matrix products, arithmetic and copies ran while one was open for 2% of the time, Pallas kernels for 0%

commit v1 on v0

v1 whole, which is shorter than its diff:
```python
import math

import jax
import jax.numpy as jnp
from jax import lax
from jax.sharding import PartitionSpec as P

COARSE = 32


def turn_rows(length, waves, col_count):
    columns = jnp.arange(col_count, dtype=jnp.int32)
    product = (waves[:, None] * columns[None, :]).astype(jnp.float32)
    len_f = length.astype(jnp.float32)
    inverse = 1.0 / len_f
    rest = product - jnp.round(product * inverse) * len_f
    half_angle = (math.pi * inverse) * rest
    square = half_angle * half_angle
    cos_half = jnp.ones_like(square)
    sin_half = jnp.ones_like(square)
    for order in range(6, 0, -1):
        cos_half = 1.0 - square * cos_half * (1.0 / ((2 * order - 1) * (2 * order)))
        sin_half = 1.0 - square * sin_half * (1.0 / ((2 * order) * (2 * order + 1)))
    sin_half = sin_half * half_angle
    return 1.0 - 2.0 * sin_half * sin_half, 2.0 * sin_half * cos_half


def local(field, target, cycle_len, legendre, spectral_filter):
    cycle_count, chan_count, col_count = field.shape
    mode_local, ring_count, degree_count = legendre.shape
    devices = ring_count // cycle_count
    mode_count = mode_local * devices
    position = lax.axis_index("lat")
    own_len = lax.dynamic_slice_in_dim(cycle_len, position * cycle_count, cycle_count)
    wavenum = jnp.arange(mode_count, dtype=jnp.int32)
    doubled = jnp.where(wavenum == 0, 1.0, 2.0).astype(jnp.float32)
    live_modes = (wavenum[None, :] < (own_len // 2)[:, None]).astype(jnp.float32)
    weight_modes = (live_modes * doubled[None])[:, None, :, None]
    columns = jnp.arange(col_count, dtype=jnp.int32)
    live_cols = (columns[None, :] < own_len[:, None])[:, None, :]

    coarse_waves = COARSE * jnp.arange(mode_count // COARSE, dtype=jnp.int32)
    fine_waves = jnp.arange(COARSE, dtype=jnp.int32)
    coarse = [turn_rows(own_len[i], coarse_waves, col_count) for i in range(cycle_count)]
    fine = [turn_rows(own_len[i], fine_waves, col_count) for i in range(cycle_count)]
    coarse, fine = lax.optimization_barrier((coarse, fine))
    tables = []
    for (cos_a, sin_a), (cos_b, sin_b) in zip(coarse, fine):
        cos_a, sin_a = cos_a[:, None, :], sin_a[:, None, :]
        cos_b, sin_b = cos_b[None], sin_b[None]
        cosine = (cos_a * cos_b - sin_a * sin_b).astype(jnp.bfloat16)
        minus_sine = (-(sin_a * cos_b) - cos_a * sin_b).astype(jnp.bfloat16)
        tables.append(
            [
                cosine.reshape(mode_count, col_count),
                minus_sine.reshape(mode_count, col_count),
            ]
        )
    tables = lax.optimization_barrier(tables)

    def analyse(values):
        return jnp.stack(
            [
                jnp.stack(
                    [
                        jnp.einsum("mj,cj->mc", tab, values[i], preferred_element_type=jnp.float32)
                        for tab in tables[i]
                    ]
                )
                for i in range(cycle_count)
            ]
        )

    live_field = jnp.where(live_cols, field, jnp.zeros_like(field))
    scale = live_modes[:, None, :, None] / own_len.astype(jnp.float32)[:, None, None, None]
    coeffs = (analyse(live_field) * scale).astype(jnp.bfloat16)
    gathered = lax.all_to_all(coeffs, "lat", split_axis=2, concat_axis=0, tiled=True)

    mode_ids = position * mode_local + jnp.arange(mode_local, dtype=jnp.int32)
    degrees = jnp.arange(degree_count, dtype=jnp.int32)
    keeper = (degrees[None, :] >= mode_ids[:, None]).astype(jnp.float32)[:, :, None, None]
    gain_table = keeper * spectral_filter[None, :, None, :]
    amplitude = jnp.einsum("mrl,rpmc->mlpc", legendre, gathered, preferred_element_type=jnp.float32)
    filtered = (amplitude * gain_table).astype(jnp.bfloat16)
    synth_modes = jnp.einsum(
        "mrl,mlpc->rpmc", legendre, filtered, preferred_element_type=jnp.float32
    ).astype(jnp.bfloat16)
    synth_back = lax.all_to_all(synth_modes, "lat", split_axis=0, concat_axis=2, tiled=True)

    weighted = (synth_back.astype(jnp.float32) * weight_modes).astype(jnp.bfloat16)
    output = jnp.stack(
        [
            sum(
                jnp.einsum("mc,mj->cj", weighted[i, p], tables[i][p], preferred_element_type=jnp.float32)
                for p in range(2)
            )
            for i in range(cycle_count)
        ]
    )
    errors = jnp.where(live_cols, output - target.astype(jnp.float32), 0.0).astype(jnp.bfloat16)

    grad_coeffs = (analyse(errors) * weight_modes).astype(jnp.bfloat16)
    grad_gathered = lax.all_to_all(grad_coeffs, "lat", split_axis=2, concat_axis=0, tiled=True)
    grad_amp = jnp.einsum(
        "mrl,rpmc->mlpc", legendre, grad_gathered, preferred_element_type=jnp.float32
    )
    filter_term = jnp.sum(amplitude * grad_amp * keeper, axis=(0, 2))
    pieces = filter_term.reshape(devices, degree_count // devices, chan_count)
    own_sum = jnp.sum(lax.all_to_all(pieces, "lat", split_axis=0, concat_axis=0, tiled=True), axis=0)
    spread = jnp.broadcast_to(own_sum[None], pieces.shape)
    grad_filter = lax.all_to_all(spread, "lat", split_axis=0, concat_axis=0, tiled=True)
    return (errors, grad_filter.reshape(degree_count, chan_count))


def solution(mesh):
    return jax.shard_map(
        local,
        mesh=mesh,
        in_specs=(
            P(("groups", "lat"), None, None),
            P(("groups", "lat"), None, None),
            P(),
            P("lat", None, None),
            P(),
        ),
        out_specs=(P(("groups", "lat"), None, None), P("groups", None)),
        check_vma=False,
    )
```

time: 888 us -> 164 us (0.18); the launches traced: 877 us -> 164 us
  matrix products: 641 us -> 46.7 us
  waiting for transfers between devices: 104 us -> 10.1 us
  blocking collectives: 23.2 us -> 72.5 us
  local copies, waits for them, and re-layouts: 49 us -> 10.1 us
  between operations: 26.3 us -> 2.43 us
    dot_general x12, matrix products: 603 us -> 11.4 us  [the longest x8 8.43 us: analyse(): jnp.einsum('mj,cj->mc', tab, values[i], preferred_element_type=jnp.float32)]
    psum x1 -> x0, waiting for transfers between devices: 83.5 us -> none  [local(): grad_filter = lax.psum(filter_term, 'lat')]
    all_to_all x0 -> x3, blocking collectives: none -> 51.2 us  [the longest x1 22.9 us: local(): lax.all_to_all(synth_modes, 'lat', split_axis=0, concat_axis=2, tiled=True)]
    rev x6 -> x0, local copies, waits for them, and re-layouts: 29.2 us -> none  [mirror_cols(): extended = jnp.concatenate([blank, values[:, ::-1], blank], axis=1)]
    all_to_all x1 -> x0, waiting for transfers between devices: 10.2 us -> none  [local(): lax.all_to_all(synth_modes, 'lat', split_axis=0, concat_axis=2, tiled=True)]
  transfers between devices with their start and end apart: 3 -> 1, of which waited for: 3 -> 1; matrix products, arithmetic and copies ran while one was open for 2% -> 4% of each run, Pallas kernels for 0% -> 0%
where the time goes in v1:
time: 164 us
  blocking collectives  72.5 us (44%)
  matrix products  46.7 us (28%)
  other arithmetic  14.6 us (9%)
  local copies, waits for them, and re-layouts  10.1 us (6%)
  waiting for transfers between devices  10.1 us (6%)
  starting transfers between devices  7.37 us (4%)
  between operations  2.43 us (1%)
    all_to_all x1, blocking collectives, local(): lax.all_to_all(synth_modes, 'lat', split_axis=0, concat_axis=2, tiled=True)  22.9 us
    all_to_all x1, blocking collectives, local(): lax.all_to_all(grad_coeffs, 'lat', split_axis=2, concat_axis=0, tiled=True)  21.3 us
    dot_general x1, matrix products, local(): jnp.einsum('mrl,mlpc->rpmc', legendre, filtered, preferred_element_type=j...  14.3 us
    all_to_all x1, blocking collectives, local(): lax.all_to_all(pieces, 'lat', split_axis=0, concat_axis=0, tiled=True)  14.2 us
    all_to_all x1, blocking collectives, local(): lax.all_to_all(spread, 'lat', split_axis=0, concat_axis=0, tiled=True)  14.1 us
    dot_general x1, matrix products, local(): jnp.einsum('mrl,rpmc->mlpc', legendre, gathered, preferred_element_type=j...  10.6 us
    dot_general x1, matrix products, local(): jnp.einsum('mrl,rpmc->mlpc', legendre, grad_gathered, preferred_element_t...  10.4 us
    all_to_all x1, waiting for transfers between devices, local(): lax.all_to_all(coeffs, 'lat', split_axis=2, concat_axis=0, tiled=True)  10.1 us
  transfers between devices with their start and end apart: 1, of which 1 were waited for; matrix products, arithmetic and copies ran while one was open for 4% of the time, Pallas kernels for 0%

profile of v1, /device:TPU:0, one launch (start us, length us, event | category | flops | bytes accessed | tf_op | source)
XLA Modules:
  0.0 163.8 jit_solution(6609896849764086019)
XLA Ops:
  0.7 0.9 and_select_fusion
  1.5 0.6 fusion.64
  3.6 0.5 multiply_multiply_fusion
  4.1 0.5 multiply_multiply_fusion.2
  4.7 0.9 multiply_multiply_fusion.4
  5.5 2.0 %subtract_convert_fusion.2 = (bf16[20,32,2688]{2,1,0:T(8,128)(2,1)S(1)}, bf16[20,32,2688]{2,1,0:T(8,128)(2,1)S(1)}) fusion(f32[32,2688]{1,0:T(8,128)S(1)} %get-tuple-element.17, f32[20,2688]{1,0:T(8,128)S(1)} %get-tuple-element.16, f32[32,2688]{1,0:T(8,128)S(1)} %get-tuple-element.15, f32[20,2688]{1,0:T(8,128)S(1)} %get-tuple-element.14), kind=kLoop, calls=%fused_computation.9 | loop fusion | flops 15482880 | bytes 7999488 | tf_op jit(solution)/shard_map/convert_element_type | solution.py:52
  7.5 2.0 %subtract_convert_fusion = (bf16[20,32,2688]{2,1,0:T(8,128)(2,1)S(1)}, bf16[20,32,2688]{2,1,0:T(8,128)(2,1)S(1)}) fusion(f32[32,2688]{1,0:T(8,128)S(1)} %get-tuple-element.21, f32[20,2688]{1,0:T(8,128)S(1)} %get-tuple-element.20, f32[32,2688]{1,0:T(8,128)S(1)} %get-tuple-element.19, f32[20,2688]{1,0:T(8,128)S(1)} %get-tuple-element.18), kind=kLoop, calls=%fused_computation.7 | loop fusion | flops 15482880 | bytes 7999488 | tf_op jit(solution)/shard_map/convert_element_type | solution.py:52
  9.5 0.4 copy-done.11
  9.9 0.2 broadcast_select_fusion
  10.1 1.1 convolution_bitcast_fusion.7
  11.1 1.1 convolution_bitcast_fusion.6
  12.2 1.1 convolution_bitcast_fusion.5
  13.3 1.1 convolution_bitcast_fusion.4
  14.5 0.2 fusion.19
  14.8 1.5 copy.20
  16.3 7.4 %all-to-all-start = ((bf16[2,2,640,128]{3,1,0,2:T(2,128)(2,1)}), bf16[2,2,640,128]{3,1,0,2:T(2,128)(2,1)S(1)}, u32[]{:S(2)}, u32[]{:S(2)}) async-start(bf16[2,2,640,128]{3,1,0,2:T(2,128)(2,1)} %copy.20), calls=%async_computation | async-start | bytes 1310720 | tf_op jit(solution)/shard_map/all_to_all | solution.py:77
  23.7 0.2 copy.22
  23.9 6.2 %broadcast_multiply_fusion = f32[40,640,128]{1,2,0:T(8,128)} fusion(f32[640,128]{0,1:T(8,128)S(1)} %copy.22, f32[40,640]{1,0:T(8,128)S(1)} %fusion.61), kind=kLoop, calls=%fused_computation.11 | loop fusion | flops 3276800 | bytes 13537280 | tf_op jit(solution)/shard_map/mul | solution.py:82
  30.2 10.1 %all-to-all-done = bf16[2,2,640,128]{3,1,0,2:T(2,128)(2,1)S(1)} async-done(((bf16[2,2,640,128]{3,1,0,2:T(2,128)(2,1)}), bf16[2,2,640,128]{3,1,0,2:T(2,128)(2,1)S(1)}, u32[]{:S(2)}, u32[]{:S(2)}) %all-to-all-start) | async-done | bytes 655392 | tf_op jit(solution)/shard_map/all_to_all | solution.py:77
  40.3 0.6 copy.21
  40.9 10.6 %fusion.12 = f32[40,2,128,640]{3,2,1,0:T(8,128)} fusion(bf16[32,2,40,128]{3,0,1,2:T(8,128)(2,1)S(1)} %bitcast.137, bf16[40,32,640]{2,1,0:T(8,128)(2,1)S(1)} %copy-done), kind=kOutput, calls=%fused_computation.21 | convolution fusion | flops 419430400 | bytes 28508160 | tf_op jit(solution)/shard_map/mrl,rpmc->mlpc/dot_general | solution.py:83
  51.5 14.3 %fusion.22 = bf16[32,2,40,128]{3,0,1,2:T(8,128)(2,1)S(1)} fusion(bf16[40,32,640]{2,1,0:T(8,128)(2,1)S(1)} %copy-done, f32[40,2,128,640]{3,2,1,0:T(8,128)} %fusion.12, f32[40,640,128]{1,2,0:T(8,128)} %broadcast_multiply_fusion), kind=kOutput, calls=%fused_computation.31 | convolution fusion | flops 432865280 | bytes 41615360 | tf_op jit(solution)/shard_map/mrl,mlpc->rpmc/dot_general | solution.py:85
  65.8 0.5 copy.24
  66.3 22.9 %all_to_all.55 = bf16[32,2,40,128]{3,1,2,0:T(2,128)(2,1)S(1)} all-to-all(bf16[32,2,40,128]{3,1,2,0:T(2,128)(2,1)S(1)} %copy.24), channel_id=1, replica_groups=mesh['groups'=2,'lat'=16] {'lat'}, dimensions={0} | all-to-all | bytes 1310720 | tf_op jit(solution)/shard_map/all_to_all | solution.py:88
  89.3 0.1 copy.25
  89.4 0.2 fusion.21
  89.6 0.8 fusion.59
  90.4 1.0 copy-done.2
  91.3 0.8 fusion.60
  92.1 1.2 copy-done.8
  93.3 0.7 fusion.7
  94.1 1.2 copy-done.4
  95.3 0.7 fusion.6
  96.0 0.6 copy-done.9
  96.6 0.3 fusion.9
  97.0 1.0 convolution_bitcast_fusion
  98.0 1.0 convolution_bitcast_fusion.2
  99.1 1.0 convolution_bitcast_fusion.1
  100.1 1.0 convolution_bitcast_fusion.3
  101.3 0.2 fusion.20
  101.5 0.7 copy.26
  102.2 21.3 %all_to_all.56 = bf16[2,2,640,128]{3,1,0,2:T(2,128)(2,1)S(1)} all-to-all(bf16[2,2,640,128]{3,1,0,2:T(2,128)(2,1)S(1)} %copy.26), channel_id=1, replica_groups=mesh['groups'=2,'lat'=16] {'lat'}, dimensions={2} | all-to-all | bytes 1310720 | tf_op jit(solution)/shard_map/all_to_all | solution.py:103
  123.5 0.6 copy.27
  124.1 10.4 %fusion.1 = f32[640,128]{0,1:T(8,128)S(1)} fusion(f32[40,2,128,640]{3,2,1,0:T(8,128)} %fusion.12, f32[40,640]{1,0:T(8,128)S(1)} %fusion.61, bf16[32,2,40,128]{3,0,1,2:T(8,128)(2,1)S(1)} %bitcast.141, bf16[40,32,640]{2,1,0:T(8,128)(2,1)S(1)} %copy-done), kind=kOutput, calls=%fused_computation.2 | convolution fusion | flops 439009280 | bytes 28938240 | tf_op jit(solution)/shard_map/mrl,rpmc->mlpc/dot_general | solution.py:104
  134.6 0.2 copy.28
  134.7 14.2 %all_to_all.57 = f32[16,40,128]{2,1,0:T(8,128)S(1)} all-to-all(f32[16,40,128]{2,1,0:T(8,128)S(1)} %bitcast.142), channel_id=1, replica_groups=mesh['groups'=2,'lat'=16] {'lat'}, dimensions={0} | all-to-all | bytes 655360 | tf_op jit(solution)/shard_map/all_to_all | solution.py:109
  149.0 14.1 %all_to_all.58 = f32[16,40,128]{2,1,0:T(8,128)S(1)} all-to-all(f32[16,40,128]{2,1,0:T(8,128)S(1)} %broadcast_in_dim.28), channel_id=1, replica_groups=mesh['groups'=2,'lat'=16] {'lat'}, dimensions={0} | all-to-all | bytes 655360 | tf_op jit(solution)/shard_map/all_to_all | solution.py:111
  163.1 0.7 copy.32
  (34 shorter events, 0.5 us)
Async XLA Ops:
  0.6 40.3 %copy-start = (bf16[40,32,640]{2,1,0:T(8,128)(2,1)S(1)}, bf16[40,32,640]{2,1,0:T(8,128)(2,1)}, u32[]{:S(2)}) copy-start(bf16[40,32,640]{2,1,0:T(8,128)(2,1)} %param.8) | copy-start | bytes 4915204
  7.5 2.6 %copy-start.1 = (bf16[20,32,2688]{2,1,0:T(8,128)(2,1)}, bf16[20,32,2688]{2,1,0:T(8,128)(2,1)S(1)}, u32[]{:S(2)}) copy-start(bf16[20,32,2688]{2,1,0:T(8,128)(2,1)S(1)} %get-tuple-element.31) | copy-start | bytes 10321924
  7.5 3.6 %copy-start.3 = (bf16[20,32,2688]{2,1,0:T(8,128)(2,1)}, bf16[20,32,2688]{2,1,0:T(8,128)(2,1)S(1)}, u32[]{:S(2)}) copy-start(bf16[20,32,2688]{2,1,0:T(8,128)(2,1)S(1)} %get-tuple-element.30) | copy-start | bytes 10321924
  7.5 2.4 %copy-start.11 = (bf16[2,128,2688]{2,1,0:T(8,128)(2,1)S(1)}, bf16[2,128,2688]{2,1,0:T(8,128)(2,1)}, u32[]{:S(2)}) copy-start(bf16[2,128,2688]{2,1,0:T(8,128)(2,1)} %param.5) | copy-start | bytes 4128772
  9.5 2.7 %copy-start.5 = (bf16[20,32,2688]{2,1,0:T(8,128)(2,1)}, bf16[20,32,2688]{2,1,0:T(8,128)(2,1)S(1)}, u32[]{:S(2)}) copy-start(bf16[20,32,2688]{2,1,0:T(8,128)(2,1)S(1)} %get-tuple-element.29) | copy-start | bytes 10321924
  9.5 3.8 %copy-start.7 = (bf16[20,32,2688]{2,1,0:T(8,128)(2,1)}, bf16[20,32,2688]{2,1,0:T(8,128)(2,1)S(1)}, u32[]{:S(2)}) copy-start(bf16[20,32,2688]{2,1,0:T(8,128)(2,1)S(1)} %get-tuple-element.28) | copy-start | bytes 10321924
  14.3 9.4 %copy-start.12 = (f32[640,128]{1,0:T(8,128)S(1)}, f32[640,128]{1,0:T(8,128)}, u32[]{:S(2)}) copy-start(f32[640,128]{1,0:T(8,128)} %param.9) | copy-start | bytes 983044
  16.3 24.0 %all-to-all-start = ((bf16[2,2,640,128]{3,1,0,2:T(2,128)(2,1)}), bf16[2,2,640,128]{3,1,0,2:T(2,128)(2,1)S(1)}, u32[]{:S(2)}, u32[]{:S(2)}) async-start(bf16[2,2,640,128]{3,1,0,2:T(2,128)(2,1)} %copy.20), calls=%async_computation | async-start | bytes 1310720 | tf_op jit(solution)/shard_map/all_to_all | solution.py:77
  65.8 23.8 %copy-start.6 = (bf16[20,32,2688]{2,1,0:T(8,128)(2,1)S(1)}, bf16[20,32,2688]{2,1,0:T(8,128)(2,1)}, u32[]{:S(2)}) copy-start(bf16[20,32,2688]{2,1,0:T(8,128)(2,1)} %copy-done.5) | copy-start | bytes 10321924
  89.4 2.0 %copy-start.2 = (bf16[20,32,2688]{2,1,0:T(8,128)(2,1)S(1)}, bf16[20,32,2688]{2,1,0:T(8,128)(2,1)}, u32[]{:S(2)}) copy-start(bf16[20,32,2688]{2,1,0:T(8,128)(2,1)} %copy-done.1) | copy-start | bytes 10321924
  91.3 2.0 %copy-start.8 = (bf16[20,32,2688]{2,1,0:T(8,128)(2,1)S(1)}, bf16[20,32,2688]{2,1,0:T(8,128)(2,1)}, u32[]{:S(2)}) copy-start(bf16[20,32,2688]{2,1,0:T(8,128)(2,1)} %copy-done.7) | copy-start | bytes 10321924
  93.3 2.0 %copy-start.4 = (bf16[20,32,2688]{2,1,0:T(8,128)(2,1)S(1)}, bf16[20,32,2688]{2,1,0:T(8,128)(2,1)}, u32[]{:S(2)}) copy-start(bf16[20,32,2688]{2,1,0:T(8,128)(2,1)} %copy-done.3) | copy-start | bytes 10321924
  95.3 1.3 copy-start.9
  97.0 3.2 %copy-start.10 = (bf16[2,128,2688]{2,1,0:T(8,128)(2,1)}, bf16[2,128,2688]{2,1,0:T(8,128)(2,1)S(1)}, u32[]{:S(2)}) copy-start(bf16[2,128,2688]{2,1,0:T(8,128)(2,1)S(1)} %fusion.9) | copy-start | bytes 4128772

commit v2 on v1

--- a/solution.py
+++ b/solution.py
@@ -1,8 +1,11 @@
+import functools
 import math
 
 import jax
 import jax.numpy as jnp
 from jax import lax
+from jax.experimental import pallas as pl
+from jax.experimental.pallas import tpu as pltpu
 from jax.sharding import PartitionSpec as P
 
 COARSE = 32
@@ -23,6 +26,112 @@
         sin_half = 1.0 - square * sin_half * (1.0 / ((2 * order) * (2 * order + 1)))
     sin_half = sin_half * half_angle
     return 1.0 - 2.0 * sin_half * sin_half, 2.0 * sin_half * cos_half
+
+
+def greet_all(count, me):
+    barrier = pltpu.get_barrier_semaphore()
+
+    @pl.loop(1, count)
+    def _(step):
+        pl.semaphore_signal(barrier, inc=1, device_id={"lat": lax.rem(me + step, count)})
+
+    pl.semaphore_wait(barrier, count - 1)
+
+
+def send_all(count, me, source_of, landing, send_sem, recv_sem):
+    @pl.loop(1, count)
+    def _(step):
+        peer = lax.rem(me + step, count)
+        pltpu.make_async_remote_copy(
+            src_ref=source_of(peer),
+            dst_ref=landing.at[me],
+            send_sem=send_sem.at[step],
+            recv_sem=recv_sem.at[step],
+            device_id={"lat": peer},
+        ).start()
+
+
+def wait_all(count, me, source_of, landing, send_sem, recv_sem):
+    @pl.loop(1, count)
+    def _(step):
+        sender = lax.rem(me + count - step, count)
+        peer = lax.rem(me + step, count)
+        copy = pltpu.make_async_remote_copy(
+            src_ref=source_of(peer),
+            dst_ref=landing.at[sender],
+            send_sem=send_sem.at[step],
+            recv_sem=recv_sem.at[step],
+            device_id={"lat": peer},
+        )
+        copy.wait_recv()
+        copy.wait_send()
+
+
+def exchange_kernel(count, x_ref, out_ref, send_sem, recv_sem):
+    me = lax.axis_index("lat")
+    greet_all(count, me)
+    send_all(count, me, lambda peer: x_ref.at[peer], out_ref, send_sem, recv_sem)
+    out_ref[me] = x_ref[me]
+    wait_all(count, me, lambda peer: x_ref.at[peer], out_ref, send_sem, recv_sem)
+
+
+def exchange(values, call_id):
+    count, rows, width = values.shape
+    padded = -(-rows // 16) * 16
+    if padded != rows:
+        values = jnp.pad(values, ((0, 0), (0, padded - rows), (0, 0)))
+    out = pl.pallas_call(
+        functools.partial(exchange_kernel, count),
+        out_shape=jax.ShapeDtypeStruct(values.shape, values.dtype),
+        in_specs=[pl.BlockSpec(memory_space=pltpu.VMEM)],
+        out_specs=pl.BlockSpec(memory_space=pltpu.VMEM),
+        scratch_shapes=[pltpu.SemaphoreType.DMA((count,)), pltpu.SemaphoreType.DMA((count,))],
+        compiler_params=pltpu.CompilerParams(
+            collective_id=call_id, has_side_effects=True, vmem_limit_bytes=16 * 2**20
+        ),
+        name=f"exchange_{call_id}",
+    )(values)
+    return out[:, :rows]
+
+
+def total_kernel(
+    count, x_ref, out_ref, landed, spread, own, send_a, recv_a, send_b, recv_b
+):
+    me = lax.axis_index("lat")
+    rows = x_ref.shape[1]
+    greet_all(count, me)
+    send_all(count, me, lambda peer: x_ref.at[peer], landed, send_a, recv_a)
+    landed[me] = x_ref[me]
+    wait_all(count, me, lambda peer: x_ref.at[peer], landed, send_a, recv_a)
+    total = jnp.sum(landed[...], axis=0)
+    blank = jnp.zeros((own.shape[0] - rows, total.shape[1]), total.dtype)
+    own[...] = jnp.concatenate([total, blank], axis=0).astype(own.dtype)
+    send_all(count, me, lambda peer: own, spread, send_b, recv_b)
+    spread[me] = own[...]
+    wait_all(count, me, lambda peer: own, spread, send_b, recv_b)
+    out_ref[...] = spread[...].astype(jnp.float32)[:, :rows]
+
+
+def total_over(pieces, call_id):
+    count, rows, width = pieces.shape
+    padded = -(-rows // 16) * 16 + (16 if rows % 16 == 0 else 0)
+    sems = [pltpu.SemaphoreType.DMA((count,)) for _ in range(4)]
+    return pl.pallas_call(
+        functools.partial(total_kernel, count),
+        out_shape=jax.ShapeDtypeStruct(pieces.shape, jnp.float32),
+        in_specs=[pl.BlockSpec(memory_space=pltpu.VMEM)],
+        out_specs=pl.BlockSpec(memory_space=pltpu.VMEM),
+        scratch_shapes=[
+            pltpu.VMEM(pieces.shape, jnp.float32),
+            pltpu.VMEM((count, padded, width), jnp.bfloat16),
+            pltpu.VMEM((padded, width), jnp.bfloat16),
+        ]
+        + sems,
+        compiler_params=pltpu.CompilerParams(
+            collective_id=call_id, has_side_effects=True, vmem_limit_bytes=16 * 2**20
+        ),
+        name="total_over",
+    )(pieces)
 
 
 def local(field, target, cycle_len, legendre, spectral_filter):
@@ -74,18 +183,29 @@
     live_field = jnp.where(live_cols, field, jnp.zeros_like(field))
     scale = live_modes[:, None, :, None] / own_len.astype(jnp.float32)[:, None, None, None]
     coeffs = (analyse(live_field) * scale).astype(jnp.bfloat16)
-    gathered = lax.all_to_all(coeffs, "lat", split_axis=2, concat_axis=0, tiled=True)
+
+    def to_modes(values, call_id):
+        split = values.reshape(cycle_count, 2, devices, mode_local, chan_count)
+        rows = split.transpose(2, 0, 1, 3, 4).reshape(devices, -1, chan_count)
+        return exchange(rows, call_id).reshape(ring_count, 2, mode_local, chan_count)
+
+    def to_cycles(values, call_id):
+        rows = exchange(values.reshape(devices, -1, chan_count), call_id)
+        split = rows.reshape(devices, cycle_count, 2, mode_local, chan_count)
+        return split.transpose(1, 2, 0, 3, 4).reshape(cycle_count, 2, mode_count, chan_count)
+
+    gathered = to_modes(coeffs, 0)
 
     mode_ids = position * mode_local + jnp.arange(mode_local, dtype=jnp.int32)
     degrees = jnp.arange(degree_count, dtype=jnp.int32)
-    keeper = (degrees[None, :] >= mode_ids[:, None]).astype(jnp.float32)[:, :, None, None]
-    gain_table = keeper * spectral_filter[None, :, None, :]
+    kept = degrees[None, None, :] >= mode_ids[:, None, None]
+    legendre = lax.optimization_barrier(jnp.where(kept, legendre, jnp.zeros_like(legendre)))
     amplitude = jnp.einsum("mrl,rpmc->mlpc", legendre, gathered, preferred_element_type=jnp.float32)
-    filtered = (amplitude * gain_table).astype(jnp.bfloat16)
+    filtered = (amplitude * spectral_filter[None, :, None, :]).astype(jnp.bfloat16)
     synth_modes = jnp.einsum(
         "mrl,mlpc->rpmc", legendre, filtered, preferred_element_type=jnp.float32
     ).astype(jnp.bfloat16)
-    synth_back = lax.all_to_all(synth_modes, "lat", split_axis=0, concat_axis=2, tiled=True)
+    synth_back = to_cycles(synth_modes, 1)
 
     weighted = (synth_back.astype(jnp.float32) * weight_modes).astype(jnp.bfloat16)
     output = jnp.stack(
@@ -100,15 +220,13 @@
     errors = jnp.where(live_cols, output - target.astype(jnp.float32), 0.0).astype(jnp.bfloat16)
 
     grad_coeffs = (analyse(errors) * weight_modes).astype(jnp.bfloat16)
-    grad_gathered = lax.all_to_all(grad_coeffs, "lat", split_axis=2, concat_axis=0, tiled=True)
+    grad_gathered = to_modes(grad_coeffs, 2)
     grad_amp = jnp.einsum(
         "mrl,rpmc->mlpc", legendre, grad_gathered, preferred_element_type=jnp.float32
     )
-    filter_term = jnp.sum(amplitude * grad_amp * keeper, axis=(0, 2))
+    filter_term = jnp.sum(amplitude * grad_amp, axis=(0, 2))
     pieces = filter_term.reshape(devices, degree_count // devices, chan_count)
-    own_sum = jnp.sum(lax.all_to_all(pieces, "lat", split_axis=0, concat_axis=0, tiled=True), axis=0)
-    spread = jnp.broadcast_to(own_sum[None], pieces.shape)
-    grad_filter = lax.all_to_all(spread, "lat", split_axis=0, concat_axis=0, tiled=True)
+    grad_filter = total_over(pieces, 3)
     return (errors, grad_filter.reshape(degree_count, chan_count))
 
 

time: 164 us -> 137 us (0.84)
  Pallas kernels: 0 us -> 77 us
  blocking collectives: 72.5 us -> 0 us
  waiting for transfers between devices: 10.1 us -> 0 us
  starting transfers between devices: 7.37 us -> 0 us
  local copies, waits for them, and re-layouts: 10.1 us -> 3.77 us
  other arithmetic: 14.6 us -> 8.72 us
  matrix products: 46.7 us -> 44.4 us
    pallas_call x0 -> x4, Pallas kernels: none -> 77 us  [the longest x3 55.4 us: exchange(): pl.pallas_call(functools.partial(exchange_kernel, count), out_shape=jax.S...]
    all_to_all x4 -> x0, blocking collectives: 72.5 us -> none  [the longest x1 22.9 us: local(): lax.all_to_all(synth_modes, 'lat', split_axis=0, concat_axis=2, tiled=True)]
    all_to_all x1 -> x0, waiting for transfers between devices: 10.1 us -> none  [local(): lax.all_to_all(coeffs, 'lat', split_axis=2, concat_axis=0, tiled=True)]
    all_to_all x1 -> x0, starting transfers between devices: 7.37 us -> none  [local(): lax.all_to_all(coeffs, 'lat', split_axis=2, concat_axis=0, tiled=True)]
    mul x1 -> x0, other arithmetic: 6.22 us -> none  [local(): gain_table = keeper * spectral_filter[None, :, None, :]]
    dot_general x1, matrix products: 14.3 us -> 11.1 us  [local(): jnp.einsum('mrl,mlpc->rpmc', legendre, filtered, preferred_element_type=j...]
    unnamed x28 -> x19, local copies, waits for them, and re-layouts: 5.29 us -> 2.55 us
    convert_element_type x2 -> x0, local copies, waits for them, and re-layouts: 2.19 us -> none  [the longest x1 1.51 us: local(): coeffs = (analyse(live_field) * scale).astype(jnp.bfloat16)]
  transfers between devices with their start and end apart: 1 -> 0, of which waited for: 1 -> 0; matrix products, arithmetic and copies ran while one was open for 4% -> 0% of each run, Pallas kernels for 0% -> 0%
where the time goes in v2:
time: 137 us; the launch traced here: 136 us
  Pallas kernels  77 us (56%)
  matrix products  44.4 us (32%)
  other arithmetic  8.72 us (6%)
  local copies, waits for them, and re-layouts  3.77 us (3%)
  between operations  2.37 us (2%)
    pallas_call x3, Pallas kernels, exchange(): pl.pallas_call(functools.partial(exchange_kernel, count), out_shape=jax.S...  55.4 us
    pallas_call x1, Pallas kernels, total_over(): pl.pallas_call(functools.partial(total_kernel, count), out_shape=jax.Shap...  21.6 us
    dot_general x1, matrix products, local(): jnp.einsum('mrl,mlpc->rpmc', legendre, filtered, preferred_element_type=j...  11.1 us
    dot_general x1, matrix products, local(): jnp.einsum('mrl,rpmc->mlpc', legendre, gathered, preferred_element_type=j...  10.6 us
    dot_general x1, matrix products, local(): jnp.einsum('mrl,rpmc->mlpc', legendre, grad_gathered, preferred_element_t...  10.4 us
    dot_general x8, matrix products, analyse(): jnp.einsum('mj,cj->mc', tab, values[i], preferred_element_type=jnp.float32)  9.26 us
    convert_element_type x2, other arithmetic, local(): minus_sine = (-(sin_a * cos_b) - cos_a * sin_b).astype(jnp.bfloat16)  4.09 us
    dot_general x4, matrix products, local(): jnp.einsum('mc,mj->cj', weighted[i, p], tables[i][p], preferred_element_t...  2.98 us

profile of v2, /device:TPU:0, one launch (start us, length us, event | category | flops | bytes accessed | tf_op | source)
XLA Modules:
  0.0 136.2 jit_solution(15853213496425194458)
XLA Ops:
  0.7 0.8 and_select_fusion
  1.5 0.6 fusion.59
  3.5 0.0 copy-start.4
  3.5 0.1 compare_select_fusion.1
  3.6 0.1 iota_compare_fusion.1
  3.7 0.1 compare_select_fusion
  3.8 0.1 iota_compare_fusion
  3.8 0.5 multiply_multiply_fusion
  4.4 0.5 multiply_multiply_fusion.2
  4.9 0.9 multiply_multiply_fusion.4
  5.8 0.2 broadcast_select_fusion.1
  6.0 0.0 copy-done.4
  6.0 0.3 broadcast_select_fusion
  6.2 2.1 %subtract_convert_fusion.2 = (bf16[20,32,2688]{2,1,0:T(8,128)(2,1)S(1)}, bf16[20,32,2688]{2,1,0:T(8,128)(2,1)S(1)}) fusion(f32[32,2688]{1,0:T(8,128)S(1)} %get-tuple-element.17, f32[20,2688]{1,0:T(8,128)S(1)} %get-tuple-element.16, f32[32,2688]{1,0:T(8,128)S(1)} %get-tuple-element.15, f32[20,2688]{1,0:T(8,128)S(1)} %get-tuple-element.14), kind=kLoop, calls=%fused_computation.6 | loop fusion | flops 15482880 | bytes 7999488 | tf_op jit(solution)/shard_map/convert_element_type | solution.py:161
  8.4 2.0 %subtract_convert_fusion = (bf16[20,32,2688]{2,1,0:T(8,128)(2,1)S(1)}, bf16[20,32,2688]{2,1,0:T(8,128)(2,1)S(1)}) fusion(f32[32,2688]{1,0:T(8,128)S(1)} %get-tuple-element.21, f32[20,2688]{1,0:T(8,128)S(1)} %get-tuple-element.20, f32[32,2688]{1,0:T(8,128)S(1)} %get-tuple-element.19, f32[20,2688]{1,0:T(8,128)S(1)} %get-tuple-element.18), kind=kLoop, calls=%fused_computation.4 | loop fusion | flops 15482880 | bytes 7999488 | tf_op jit(solution)/shard_map/convert_element_type | solution.py:161
  10.4 1.2 convolution_bitcast_fusion.6
  11.5 1.2 convolution_bitcast_fusion.7
  12.7 1.2 convolution_bitcast_fusion.5
  13.9 1.1 convolution_bitcast_fusion.4
  15.0 0.2 fusion.20
  15.3 0.1 copy.12
  15.3 17.5 %exchange_0.1 = bf16[16,160,128]{2,1,0:T(8,128)(2,1)S(1)} custom-call(bf16[16,160,128]{2,1,0:T(8,128)(2,1)S(1)} %bitcast.109), custom_call_target="tpu_custom_call" | custom-call | tf_op jit(solution)/shard_map/exchange_0/pallas_call | solution.py:83
  32.8 0.0 copy-start.8
  32.8 10.6 %fusion.8 = f32[40,640,2,128]{3,1,2,0:T(8,128)} fusion(bf16[40,32,640]{2,1,0:T(8,128)(2,1)S(1)} %broadcast_select_fusion, bf16[32,2,40,128]{3,2,1,0:T(8,128)(2,1)S(1)} %bitcast.108), kind=kOutput, calls=%fused_computation.17 | convolution fusion | flops 419430400 | bytes 28508160 | tf_op jit(solution)/shard_map/mrl,rpmc->mlpc/dot_general | solution.py:203
  43.4 11.1 %fusion.16 = bf16[32,2,40,128]{3,0,1,2:T(8,128)(2,1)S(1)} fusion(f32[40,640,2,128]{3,1,2,0:T(8,128)} %fusion.8, f32[640,128]{1,0:T(8,128)S(1)} %copy-done.8, bf16[40,32,640]{2,1,0:T(8,128)(2,1)S(1)} %broadcast_select_fusion), kind=kOutput, calls=%fused_computation.28 | convolution fusion | flops 432865280 | bytes 28835840 | tf_op jit(solution)/shard_map/mrl,mlpc->rpmc/dot_general | solution.py:205
  54.6 0.4 copy.14
  55.0 18.9 %exchange_1.1 = bf16[16,160,128]{2,1,0:T(8,128)(2,1)S(1)} custom-call(bf16[16,160,128]{2,1,0:T(8,128)(2,1)S(1)} %bitcast.110), custom_call_target="tpu_custom_call" | custom-call | tf_op jit(solution)/shard_map/exchange_1/pallas_call | solution.py:83
  73.9 0.1 copy.15
  74.0 0.2 fusion.15
  74.2 0.7 fusion.55
  75.0 1.2 copy-done.3
  76.2 0.7 fusion.3
  76.9 0.7 fusion.56
  77.7 0.0 copy-start.5
  77.7 0.7 fusion.2
  78.5 0.6 copy-done.5
  79.0 0.4 fusion.5
  79.4 0.0 copy-start.6
  79.4 1.2 convolution_bitcast_fusion
  80.6 1.2 convolution_bitcast_fusion.2
  81.8 1.2 convolution_bitcast_fusion.1
  82.9 1.2 convolution_bitcast_fusion.3
  84.1 0.2 fusion.19
  84.3 0.1 copy.16
  84.4 19.1 %exchange_2.1 = bf16[16,160,128]{2,1,0:T(8,128)(2,1)S(1)} custom-call(bf16[16,160,128]{2,1,0:T(8,128)(2,1)S(1)} %bitcast.111), custom_call_target="tpu_custom_call" | custom-call | tf_op jit(solution)/shard_map/exchange_2/pallas_call | solution.py:83
  103.5 10.4 %multiply_reduce_fusion = f32[640,128]{1,0:T(8,128)S(1)} fusion(f32[40,640,2,128]{3,1,2,0:T(8,128)} %fusion.8, bf16[40,32,640]{2,1,0:T(8,128)(2,1)S(1)} %broadcast_select_fusion, bf16[32,2,40,128]{3,2,1,0:T(8,128)(2,1)S(1)} %bitcast.113), kind=kOutput, calls=%fused_computation | convolution fusion | flops 432455680 | bytes 28835840 | tf_op jit(solution)/shard_map/mrl,rpmc->mlpc/dot_general | solution.py:224
  113.9 21.6 %total_over.1 = f32[16,40,128]{2,1,0:T(8,128)S(1)} custom-call(f32[16,40,128]{2,1,0:T(8,128)S(1)} %bitcast.114), custom_call_target="tpu_custom_call" | custom-call | tf_op jit(solution)/shard_map/total_over/pallas_call | solution.py:119
  135.5 0.7 copy.24
  (17 shorter events, 0.1 us)
Async XLA Ops:
  0.6 5.2 %copy-start.7 = (bf16[2,128,2688]{2,1,0:T(8,128)(2,1)S(1)}, bf16[2,128,2688]{2,1,0:T(8,128)(2,1)}, u32[]{:S(2)}) copy-start(bf16[2,128,2688]{2,1,0:T(8,128)(2,1)} %param.5) | copy-start | bytes 4128772
  3.5 2.5 %copy-start.4 = (bf16[40,32,640]{2,1,0:T(8,128)(2,1)S(1)}, bf16[40,32,640]{2,1,0:T(8,128)(2,1)}, u32[]{:S(2)}) copy-start(bf16[40,32,640]{2,1,0:T(8,128)(2,1)} %param.8) | copy-start | bytes 4915204
  10.3 2.4 %copy-start = (bf16[20,32,2688]{2,1,0:T(8,128)(2,1)}, bf16[20,32,2688]{2,1,0:T(8,128)(2,1)S(1)}, u32[]{:S(2)}) copy-start(bf16[20,32,2688]{2,1,0:T(8,128)(2,1)S(1)} %get-tuple-element.29) | copy-start | bytes 10321924
  10.4 3.5 %copy-start.2 = (bf16[20,32,2688]{2,1,0:T(8,128)(2,1)}, bf16[20,32,2688]{2,1,0:T(8,128)(2,1)S(1)}, u32[]{:S(2)}) copy-start(bf16[20,32,2688]{2,1,0:T(8,128)(2,1)S(1)} %get-tuple-element.28) | copy-start | bytes 10321924
  32.8 10.6 %copy-start.8 = (f32[640,128]{1,0:T(8,128)S(1)}, f32[640,128]{1,0:T(8,128)}, u32[]{:S(2)}) copy-start(f32[640,128]{1,0:T(8,128)} %param.9) | copy-start | bytes 983044
  55.0 19.2 %copy-start.1 = (bf16[20,32,2688]{2,1,0:T(8,128)(2,1)S(1)}, bf16[20,32,2688]{2,1,0:T(8,128)(2,1)}, u32[]{:S(2)}) copy-start(bf16[20,32,2688]{2,1,0:T(8,128)(2,1)} %copy-done) | copy-start | bytes 10321924
  74.2 2.0 %copy-start.3 = (bf16[20,32,2688]{2,1,0:T(8,128)(2,1)S(1)}, bf16[20,32,2688]{2,1,0:T(8,128)(2,1)}, u32[]{:S(2)}) copy-start(bf16[20,32,2688]{2,1,0:T(8,128)(2,1)} %copy-done.2) | copy-start | bytes 10321924
  77.7 1.3 copy-start.5
  79.4 3.5 %copy-start.6 = (bf16[2,128,2688]{2,1,0:T(8,128)(2,1)}, bf16[2,128,2688]{2,1,0:T(8,128)(2,1)S(1)}, u32[]{:S(2)}) copy-start(bf16[2,128,2688]{2,1,0:T(8,128)(2,1)S(1)} %fusion.5) | copy-start | bytes 4128772

commit v3 on v2

--- a/solution.py
+++ b/solution.py
@@ -98,14 +98,12 @@
     count, x_ref, out_ref, landed, spread, own, send_a, recv_a, send_b, recv_b
 ):
     me = lax.axis_index("lat")
-    rows = x_ref.shape[1]
+    rows = out_ref.shape[1]
     greet_all(count, me)
     send_all(count, me, lambda peer: x_ref.at[peer], landed, send_a, recv_a)
     landed[me] = x_ref[me]
     wait_all(count, me, lambda peer: x_ref.at[peer], landed, send_a, recv_a)
-    total = jnp.sum(landed[...], axis=0)
-    blank = jnp.zeros((own.shape[0] - rows, total.shape[1]), total.dtype)
-    own[...] = jnp.concatenate([total, blank], axis=0).astype(own.dtype)
+    own[...] = jnp.sum(landed[...].astype(jnp.float32), axis=0).astype(own.dtype)
     send_all(count, me, lambda peer: own, spread, send_b, recv_b)
     spread[me] = own[...]
     wait_all(count, me, lambda peer: own, spread, send_b, recv_b)
@@ -114,7 +112,8 @@
 
 def total_over(pieces, call_id):
     count, rows, width = pieces.shape
-    padded = -(-rows // 16) * 16 + (16 if rows % 16 == 0 else 0)
+    padded = -(-rows // 16) * 16
+    terms = jnp.pad(pieces, ((0, 0), (0, padded - rows), (0, 0))).astype(jnp.bfloat16)
     sems = [pltpu.SemaphoreType.DMA((count,)) for _ in range(4)]
     return pl.pallas_call(
         functools.partial(total_kernel, count),
@@ -122,7 +121,7 @@
         in_specs=[pl.BlockSpec(memory_space=pltpu.VMEM)],
         out_specs=pl.BlockSpec(memory_space=pltpu.VMEM),
         scratch_shapes=[
-            pltpu.VMEM(pieces.shape, jnp.float32),
+            pltpu.VMEM((count, padded, width), jnp.bfloat16),
             pltpu.VMEM((count, padded, width), jnp.bfloat16),
             pltpu.VMEM((padded, width), jnp.bfloat16),
         ]
@@ -131,7 +130,7 @@
             collective_id=call_id, has_side_effects=True, vmem_limit_bytes=16 * 2**20
         ),
         name="total_over",
-    )(pieces)
+    )(terms)
 
 
 def local(field, target, cycle_len, legendre, spectral_filter):

time: 137 us -> 134 us (0.978)
  Pallas kernels: 77 us -> 74.4 us
    pallas_call x1, Pallas kernels: 21.6 us -> 19 us  [total_over(): pl.pallas_call(functools.partial(total_kernel, count), out_shape=jax.Shap...]
where the time goes in v3:
time: 134 us
  Pallas kernels  74.4 us (56%)
  matrix products  44.4 us (33%)
  other arithmetic  8.72 us (7%)
  local copies, waits for them, and re-layouts  3.79 us (3%)
  between operations  2.38 us (2%)
    pallas_call x3, Pallas kernels, exchange(): pl.pallas_call(functools.partial(exchange_kernel, count), out_shape=jax.S...  55.4 us
    pallas_call x1, Pallas kernels, total_over(): pl.pallas_call(functools.partial(total_kernel, count), out_shape=jax.Shap...  19 us
    dot_general x1, matrix products, local(): jnp.einsum('mrl,mlpc->rpmc', legendre, filtered, preferred_element_type=j...  11.1 us
    dot_general x1, matrix products, local(): jnp.einsum('mrl,rpmc->mlpc', legendre, gathered, preferred_element_type=j...  10.6 us
    dot_general x1, matrix products, local(): jnp.einsum('mrl,rpmc->mlpc', legendre, grad_gathered, preferred_element_t...  10.4 us
    dot_general x8, matrix products, analyse(): jnp.einsum('mj,cj->mc', tab, values[i], preferred_element_type=jnp.float32)  9.26 us
    convert_element_type x2, other arithmetic, local(): minus_sine = (-(sin_a * cos_b) - cos_a * sin_b).astype(jnp.bfloat16)  4.09 us
    dot_general x4, matrix products, local(): jnp.einsum('mc,mj->cj', weighted[i, p], tables[i][p], preferred_element_t...  2.98 us

profile of v3, /device:TPU:0, one launch (start us, length us, event | category | flops | bytes accessed | tf_op | source)
XLA Modules:
  0.0 133.7 jit_solution(6847592077676016897)
XLA Ops:
  0.7 0.8 and_select_fusion
  1.5 0.6 fusion.59
  3.5 0.0 copy-start.4
  3.5 0.1 compare_select_fusion.1
  3.6 0.1 iota_compare_fusion.1
  3.7 0.1 compare_select_fusion
  3.8 0.1 iota_compare_fusion
  3.8 0.5 multiply_multiply_fusion
  4.4 0.5 multiply_multiply_fusion.2
  4.9 0.9 multiply_multiply_fusion.4
  5.8 0.2 broadcast_select_fusion.1
  6.0 0.0 copy-done.4
  6.0 0.3 broadcast_select_fusion
  6.2 2.1 %subtract_convert_fusion.2 = (bf16[20,32,2688]{2,1,0:T(8,128)(2,1)S(1)}, bf16[20,32,2688]{2,1,0:T(8,128)(2,1)S(1)}) fusion(f32[32,2688]{1,0:T(8,128)S(1)} %get-tuple-element.17, f32[20,2688]{1,0:T(8,128)S(1)} %get-tuple-element.16, f32[32,2688]{1,0:T(8,128)S(1)} %get-tuple-element.15, f32[20,2688]{1,0:T(8,128)S(1)} %get-tuple-element.14), kind=kLoop, calls=%fused_computation.6 | loop fusion | flops 15482880 | bytes 7999488 | tf_op jit(solution)/shard_map/convert_element_type | solution.py:160
  8.4 2.0 %subtract_convert_fusion = (bf16[20,32,2688]{2,1,0:T(8,128)(2,1)S(1)}, bf16[20,32,2688]{2,1,0:T(8,128)(2,1)S(1)}) fusion(f32[32,2688]{1,0:T(8,128)S(1)} %get-tuple-element.21, f32[20,2688]{1,0:T(8,128)S(1)} %get-tuple-element.20, f32[32,2688]{1,0:T(8,128)S(1)} %get-tuple-element.19, f32[20,2688]{1,0:T(8,128)S(1)} %get-tuple-element.18), kind=kLoop, calls=%fused_computation.4 | loop fusion | flops 15482880 | bytes 7999488 | tf_op jit(solution)/shard_map/convert_element_type | solution.py:160
  10.4 1.2 convolution_bitcast_fusion.6
  11.5 1.2 convolution_bitcast_fusion.7
  12.7 1.2 convolution_bitcast_fusion.5
  13.9 1.1 convolution_bitcast_fusion.4
  15.0 0.2 fusion.20
  15.3 0.1 copy.12
  15.3 17.5 %exchange_0.1 = bf16[16,160,128]{2,1,0:T(8,128)(2,1)S(1)} custom-call(bf16[16,160,128]{2,1,0:T(8,128)(2,1)S(1)} %bitcast.109), custom_call_target="tpu_custom_call" | custom-call | tf_op jit(solution)/shard_map/exchange_0/pallas_call | solution.py:83
  32.8 0.0 copy-start.8
  32.8 10.6 %fusion.8 = f32[40,640,2,128]{3,1,2,0:T(8,128)} fusion(bf16[40,32,640]{2,1,0:T(8,128)(2,1)S(1)} %broadcast_select_fusion, bf16[32,2,40,128]{3,2,1,0:T(8,128)(2,1)S(1)} %bitcast.108), kind=kOutput, calls=%fused_computation.17 | convolution fusion | flops 419430400 | bytes 28508160 | tf_op jit(solution)/shard_map/mrl,rpmc->mlpc/dot_general | solution.py:202
  43.4 11.1 %fusion.16 = bf16[32,2,40,128]{3,0,1,2:T(8,128)(2,1)S(1)} fusion(f32[40,640,2,128]{3,1,2,0:T(8,128)} %fusion.8, f32[640,128]{1,0:T(8,128)S(1)} %copy-done.8, bf16[40,32,640]{2,1,0:T(8,128)(2,1)S(1)} %broadcast_select_fusion), kind=kOutput, calls=%fused_computation.28 | convolution fusion | flops 432865280 | bytes 28835840 | tf_op jit(solution)/shard_map/mrl,mlpc->rpmc/dot_general | solution.py:204
  54.6 0.4 copy.14
  55.0 18.9 %exchange_1.1 = bf16[16,160,128]{2,1,0:T(8,128)(2,1)S(1)} custom-call(bf16[16,160,128]{2,1,0:T(8,128)(2,1)S(1)} %bitcast.110), custom_call_target="tpu_custom_call" | custom-call | tf_op jit(solution)/shard_map/exchange_1/pallas_call | solution.py:83
  73.9 0.1 copy.15
  74.0 0.2 fusion.15
  74.2 0.7 fusion.55
  75.0 1.2 copy-done.3
  76.2 0.7 fusion.3
  76.9 0.7 fusion.56
  77.7 0.0 copy-start.5
  77.7 0.7 fusion.2
  78.5 0.6 copy-done.5
  79.0 0.4 fusion.5
  79.4 0.0 copy-start.6
  79.4 1.2 convolution_bitcast_fusion
  80.6 1.2 convolution_bitcast_fusion.2
  81.8 1.2 convolution_bitcast_fusion.1
  82.9 1.2 convolution_bitcast_fusion.3
  84.1 0.2 fusion.19
  84.3 0.1 copy.16
  84.4 19.1 %exchange_2.1 = bf16[16,160,128]{2,1,0:T(8,128)(2,1)S(1)} custom-call(bf16[16,160,128]{2,1,0:T(8,128)(2,1)S(1)} %bitcast.111), custom_call_target="tpu_custom_call" | custom-call | tf_op jit(solution)/shard_map/exchange_2/pallas_call | solution.py:83
  103.5 10.4 %multiply_reduce_fusion = bf16[640,128]{1,0:T(8,128)(2,1)S(1)} fusion(f32[40,640,2,128]{3,1,2,0:T(8,128)} %fusion.8, bf16[40,32,640]{2,1,0:T(8,128)(2,1)S(1)} %broadcast_select_fusion, bf16[32,2,40,128]{3,2,1,0:T(8,128)(2,1)S(1)} %bitcast.113), kind=kOutput, calls=%fused_computation | convolution fusion | flops 432455680 | bytes 28672000 | tf_op jit(solution)/shard_map/mrl,rpmc->mlpc/dot_general | solution.py:223
  113.9 19.0 %total_over.1 = f32[16,40,128]{2,1,0:T(8,128)S(1)} custom-call(bf16[16,48,128]{2,1,0:T(8,128)(2,1)S(1)} %pad.5.x_ref), custom_call_target="tpu_custom_call" | custom-call | tf_op jit(solution)/shard_map/total_over/pallas_call | solution.py:118
  132.9 0.7 copy.24
  (18 shorter events, 0.1 us)
Async XLA Ops:
  0.6 5.2 %copy-start.7 = (bf16[2,128,2688]{2,1,0:T(8,128)(2,1)S(1)}, bf16[2,128,2688]{2,1,0:T(8,128)(2,1)}, u32[]{:S(2)}) copy-start(bf16[2,128,2688]{2,1,0:T(8,128)(2,1)} %param.5) | copy-start | bytes 4128772
  3.5 2.5 %copy-start.4 = (bf16[40,32,640]{2,1,0:T(8,128)(2,1)S(1)}, bf16[40,32,640]{2,1,0:T(8,128)(2,1)}, u32[]{:S(2)}) copy-start(bf16[40,32,640]{2,1,0:T(8,128)(2,1)} %param.8) | copy-start | bytes 4915204
  10.3 2.4 %copy-start = (bf16[20,32,2688]{2,1,0:T(8,128)(2,1)}, bf16[20,32,2688]{2,1,0:T(8,128)(2,1)S(1)}, u32[]{:S(2)}) copy-start(bf16[20,32,2688]{2,1,0:T(8,128)(2,1)S(1)} %get-tuple-element.29) | copy-start | bytes 10321924
  10.4 3.5 %copy-start.2 = (bf16[20,32,2688]{2,1,0:T(8,128)(2,1)}, bf16[20,32,2688]{2,1,0:T(8,128)(2,1)S(1)}, u32[]{:S(2)}) copy-start(bf16[20,32,2688]{2,1,0:T(8,128)(2,1)S(1)} %get-tuple-element.28) | copy-start | bytes 10321924
  32.8 10.6 %copy-start.8 = (f32[640,128]{1,0:T(8,128)S(1)}, f32[640,128]{1,0:T(8,128)}, u32[]{:S(2)}) copy-start(f32[640,128]{1,0:T(8,128)} %param.9) | copy-start | bytes 983044
  55.0 19.2 %copy-start.1 = (bf16[20,32,2688]{2,1,0:T(8,128)(2,1)S(1)}, bf16[20,32,2688]{2,1,0:T(8,128)(2,1)}, u32[]{:S(2)}) copy-start(bf16[20,32,2688]{2,1,0:T(8,128)(2,1)} %copy-done) | copy-start | bytes 10321924
  74.2 2.0 %copy-start.3 = (bf16[20,32,2688]{2,1,0:T(8,128)(2,1)S(1)}, bf16[20,32,2688]{2,1,0:T(8,128)(2,1)}, u32[]{:S(2)}) copy-start(bf16[20,32,2688]{2,1,0:T(8,128)(2,1)} %copy-done.2) | copy-start | bytes 10321924
  77.7 1.3 %copy-start.5 = (bf16[2,128,2688]{2,1,0:T(8,128)(2,1)S(1)}, bf16[2,128,2688]{2,1,0:T(8,128)(2,1)}, u32[]{:S(2)}) copy-start(bf16[2,128,2688]{2,1,0:T(8,128)(2,1)} %param.6) | copy-start | bytes 4128772
  79.4 3.5 %copy-start.6 = (bf16[2,128,2688]{2,1,0:T(8,128)(2,1)}, bf16[2,128,2688]{2,1,0:T(8,128)(2,1)S(1)}, u32[]{:S(2)}) copy-start(bf16[2,128,2688]{2,1,0:T(8,128)(2,1)S(1)} %fusion.5) | copy-start | bytes 4128772
